TPU v7x, 128 devices: a whole 4x4x4 slice. The times are simulated.
128 devices in a mesh: ctx: 16 (over z, y), tp: 8 (over x, core).
Axes of the slice: x: 4, y: 4, z: 4, core: 2. Of those that a mesh axis runs over, the one named last changes fastest.
Arguments:
- queries: bfloat16 [2048, 8192], P('ctx', 'tp'), may hold values from -240 to 240
- stored_key_rows: bfloat16 [32768, 1024], P('ctx', 'tp'), may hold values from -12 to 12
- stored_value_rows: bfloat16 [32768, 1024], P('ctx', 'tp'), may hold values from -6 to 6
- fresh_key_rows: bfloat16 [2048, 1024], P('ctx', 'tp'), may hold values from -12 to 12
- fresh_value_rows: bfloat16 [2048, 1024], P('ctx', 'tp'), may hold values from -6 to 6
- cached_slot_position: int32 [32768], P('ctx'), may hold values from 0 to 32767, each once
- new_order: int32 [2048], P('ctx'), may hold values from 0 to 2047, each once
- span_len: int32 [16], P('ctx'), may hold values from 0 to 128
Outputs:
- attended: bfloat16 [2048, 8192], P('ctx', 'tp')
- mass: float32 [2048, 64], P('ctx', 'tp')
Inputs may be any that keep to these rules, and one draw needn't show every extreme that they name: cached_slot_position holds every position below 32768 once. new_order holds every place below 2048 once.
All inputs are finite; a program needn't handle non-finite values.
Results may differ from a plain program's by a relative error of at most 0.024.
Values may be sent and summed in bfloat16 or wider, within the bound.
No kernel may reach another device: no remote copies, remote signals or barrier semaphores. Data moves between devices by JAX's collectives and lax.ppermute only.
A program may use at most 128 MiB of HBM per device.

v0:
```python
import functools

import jax
import jax.numpy as jnp
import ml_dtypes
import numpy as np
from jax import lax
from jax.experimental import pallas as pl
from jax.experimental.pallas import tpu as pltpu
from jax.sharding import PartitionSpec as P

GROUP = 8
HEAD = 128
TOK = 128
ROWS = GROUP * TOK
CACHED = 32768
SIDE = 4
CHUNK = 1024
TP = 8
KT = 256
LOG2E = 1.4426950408889634
LN2 = 0.6931471805599453
LOW = -1e30
TOO_BIG = 2.0**100
TOO_SMALL = 2.0**-60
META = 16

VMEM = pl.BlockSpec(memory_space=pltpu.VMEM)


def shift(block, kind, step):
    pairs = []
    for i in range(SIDE * SIDE):
        z, y = divmod(i, SIDE)
        for t in range(TP):
            if (t % 2 == 0) == (kind == "keys"):
                j = z * SIDE + (y + step) % SIDE
            else:
                j = ((z + step) % SIDE) * SIDE + y
            pairs.append((i * TP + t, j * TP + t))
    return lax.ppermute(block, ("ctx", "tp"), pairs)


def _bf(x):
    return np.asarray(x, np.float32).astype(ml_dtypes.bfloat16).astype(np.float64)


def _fit():
    t = np.cos(np.linspace(0, np.pi, 4001)) * 0.5
    u = t * t
    cos = np.polynomial.polynomial.polyfit(u, np.cos(2 * np.pi * t), 8)
    good = np.abs(t) > 1e-3
    sin = np.polynomial.polynomial.polyfit(u[good], np.sin(2 * np.pi * t[good]) / t[good], 7)
    return [float(c) for c in cos], [float(c) for c in sin]


COS, SIN = _fit()


def _turns():
    turns = 500000.0 ** (-2.0 * np.arange(64) / HEAD) / (2 * np.pi)
    first = _bf(turns)
    second = _bf(turns - first)
    return [[float(x) for x in piece] for piece in (first, second, turns - first - second)]


TURNS = _turns()


def spread(constants):
    row = lax.broadcasted_iota(jnp.int32, (8, TOK), 0)
    tiles = []
    for first in range(0, 64, 8):
        tile = jnp.full((8, TOK), constants[first + 7], jnp.float32)
        for i in range(7):
            tile = jnp.where(row == i, constants[first + i], tile)
        tiles.append(tile)
    return jnp.concatenate(tiles, 0)


def angles(positions, turns):
    a = positions * turns[0]
    a = a - jnp.round(a)
    b = positions * turns[1]
    t = a + (b - jnp.round(b)) + positions * turns[2]
    t = t - jnp.round(t)
    u = t * t
    cos = jnp.full_like(u, COS[-1])
    for c in COS[-2::-1]:
        cos = cos * u + c
    sin = jnp.full_like(u, SIN[-1])
    for c in SIN[-2::-1]:
        sin = sin * u + c
    return cos, sin * t


def turned(x, cos, sin):
    lower, upper = x[:64], x[64:]
    return jnp.concatenate([lower * cos - upper * sin, upper * cos + lower * sin], 0)


def coded(places):
    high = jnp.right_shift(places, 4)
    rows = lax.broadcasted_iota(jnp.int32, (META, TOK), 0)
    both = jnp.where(rows == 0, high, jnp.where(rows == 1, places - high * 16, 0))
    return both.astype(jnp.float32).astype(jnp.bfloat16)


def places_of(meta):
    meta = meta.astype(jnp.float32)
    return meta[0:1, :] * 16.0 + meta[1:2, :]


def angle_kernel(order_ref, out_ref):
    order = order_ref[...]
    turns = [spread(piece) for piece in TURNS]
    cos, sin = angles((order + CACHED).astype(jnp.float32), turns)
    scale = HEAD**-0.5 * LOG2E
    out_ref[0:64, :] = cos * scale
    out_ref[64:128, :] = sin * scale
    out_ref[128:, :] = coded(order).astype(jnp.float32)


def query_kernel(q_ref, angle_ref, out_ref):
    cos, sin = angle_ref[0:64, :], angle_ref[64:128, :]
    for g in range(GROUP):
        lanes = slice(g * HEAD, (g + 1) * HEAD)
        x = q_ref[:, lanes].astype(jnp.float32).T
        out_ref[0:HEAD, lanes] = turned(x, cos, sin).astype(jnp.bfloat16)
    out_ref[HEAD:, :] = jnp.concatenate([angle_ref[128:, :].astype(jnp.bfloat16)] * GROUP, 1)


FRESH_KEYS = 2 * CHUNK
FRESH_VALUES = FRESH_KEYS + TOK
PLACES = FRESH_VALUES + TOK


def key_kernel(start, k_ref, v_ref, pos_ref, *refs):
    with_fresh = len(refs) > 1
    if with_fresh:
        fk_ref, fv_ref, order_ref, span_ref, out_ref = refs
    else:
        (out_ref,) = refs
    turns = [spread(piece) for piece in TURNS]

    def keys(x, positions):
        cos, sin = angles(positions.astype(jnp.float32), turns)
        return turned(x.astype(jnp.float32).T, cos, sin).T.astype(jnp.bfloat16)

    def values(x):
        return x.astype(jnp.float32).T.astype(jnp.bfloat16)

    for b in range(CHUNK // TOK):
        rows = slice(start + b * TOK, start + (b + 1) * TOK)
        tile = start // TOK + b
        out_ref[b * TOK : (b + 1) * TOK, :] = keys(k_ref[rows, :], pos_ref[tile : tile + 1, :])
        out_ref[CHUNK + b * TOK : CHUNK + (b + 1) * TOK, :] = values(v_ref[rows, :])
    if with_fresh:
        order = order_ref[...]
        out_ref[FRESH_KEYS:FRESH_VALUES, :] = keys(fk_ref[...], order + CACHED)
        out_ref[FRESH_VALUES:PLACES, :] = values(fv_ref[...])
        lane = lax.broadcasted_iota(jnp.int32, (1, TOK), 1)
        out_ref[PLACES:, :] = coded(jnp.where(lane < span_ref[0], order, 4000))


def dot(a, b):
    return lax.dot_general(a, b, (((1,), (0,)), ((), ())), preferred_element_type=jnp.float32)


def attend_kernel(plan, *refs):
    it = iter(refs)
    n_q, n_fresh = plan["n_q"], plan["n_fresh"]
    q_refs = [next(it) for _ in range(n_q)]
    kv_refs = [next(it) for _ in range(plan["n_kv"])]
    fresh_refs = [next(it) for _ in range(n_fresh)]
    if not plan["start"]:
        acc_in, ml_in = next(it), next(it)
    if plan["finish"]:
        out_refs = [next(it) for _ in range(n_q)]
    else:
        acc_out, ml_out = next(it), next(it)
    q_s = next(it)
    if n_fresh:
        f_s, place_s = next(it), next(it)
    if plan["finish"]:
        acc_out, ml_out = next(it), next(it)

    for i, r in enumerate(q_refs):
        q_s[i] = r[...]
    for i, r in enumerate(fresh_refs):
        f_s[i * TOK : (i + 1) * TOK, :] = r[FRESH_KEYS:FRESH_VALUES, :]
        f_s[(n_fresh + i) * TOK : (n_fresh + i + 1) * TOK, :] = r[FRESH_VALUES:PLACES, :]
        place_s[i * TOK : (i + 1) * TOK, :] = jnp.broadcast_to(places_of(r[PLACES:, :]), (TOK, TOK)).T

    def aligned(i):
        return i if isinstance(i, int) else pl.multiple_of(i, TOK)

    def k_tile(ref, first):
        return ref[pl.ds(aligned(first), KT), :]

    def v_tile(ref, first):
        return jnp.concatenate([ref[pl.ds(aligned(first + j * TOK), TOK), :] for j in range(KT // TOK)], 1)

    def scores(ref, first, item, masked):
        s = dot(k_tile(ref, first), q_s[item, 0:HEAD, :])
        if masked:
            mine = places_of(q_s[item, HEAD:, 0:TOK])
            mask = place_s[pl.ds(aligned(first), KT), :] <= mine
            s = jnp.where(jnp.concatenate([mask] * GROUP, 1), s, LOW)
        return s

    sources = [(ref, CHUNK, CHUNK, False) for ref in kv_refs]
    if n_fresh:
        sources.append((f_s, n_fresh * TOK, n_fresh * TOK, True))

    def old_of(item):
        if plan["start"]:
            return None
        at = item + plan["skip"]
        return ml_in[at][0:1, :], ml_in[at][1:2, :], acc_in[at]

    skip = plan["skip"]

    def put(item, m, total, acc):
        acc_out[item] = acc
        ml_out[item] = jnp.concatenate([m, total, jnp.zeros((6, ROWS), jnp.float32)], 0)

    def quick(item):
        tiles = [(ref, first, values, masked) for ref, values, n, masked in sources for first in range(0, n, KT)]
        old = old_of(item)
        if old is None:
            m, total, acc = None, None, None
        else:
            m, total, acc = old
        part = jnp.zeros((8, ROWS), jnp.float32)

        def scores_of(tile):
            return scores(tile[0], tile[1], item, tile[3])

        ahead = scores_of(tiles[0])
        for j, (ref, first, values, _) in enumerate(tiles):
            s = ahead
            if j + 1 < len(tiles):
                ahead = scores_of(tiles[j + 1])
            p = jnp.exp2(s) if m is None else jnp.exp2(s - m)
            part = part + jnp.sum(p.reshape(KT // 8, 8, ROWS), 0)
            pv = dot(v_tile(ref, values + first), p.astype(jnp.bfloat16))
            acc = pv if acc is None else acc + pv
        part = jnp.sum(part, 0, keepdims=True)
        if m is None:
            m, total = jnp.zeros((1, ROWS), jnp.float32), part
        else:
            total = total + part
        put(item, m, total, acc)

    def careful(item):
        def group(g, carry):
            lanes = pl.ds(aligned(g * TOK), TOK)
            if plan["start"]:
                m = jnp.full((1, TOK), LOW, jnp.float32)
                total = jnp.zeros((1, TOK), jnp.float32)
                acc = jnp.zeros((HEAD, TOK), jnp.float32)
            else:
                at = item + skip
                m, total, acc = ml_in[at, 0:1, lanes], ml_in[at, 1:2, lanes], acc_in[at, :, lanes]
            q = q_s[item, 0:HEAD, lanes]
            for ref, values, n, masked in sources:

                def step(t, state, ref=ref, values=values, masked=masked):
                    m, total, acc = state
                    first = t * KT
                    s = dot(k_tile(ref, first), q)
                    if masked:
                        mine = places_of(q_s[item, HEAD:, 0:TOK])
                        s = jnp.where(place_s[pl.ds(aligned(first), KT), :] <= mine, s, LOW)
                    top = jnp.maximum(m, jnp.max(s, 0, keepdims=True))
                    back = jnp.exp2(m - top)
                    p = jnp.where(s > 0.5 * LOW, jnp.exp2(s - top), 0.0)
                    total = total * back + jnp.sum(p, 0, keepdims=True)
                    acc = acc * back + dot(v_tile(ref, values + first), p.astype(jnp.bfloat16))
                    return top, total, acc

                m, total, acc = lax.fori_loop(0, n // KT, step, (m, total, acc))
            acc_out[item, :, lanes] = acc
            ml_out[item, 0:1, lanes] = m
            ml_out[item, 1:2, lanes] = total
            return carry

        lax.fori_loop(0, GROUP, group, 0)

    def everything(step):
        def body(item, carry):
            step(item)
            return carry

        if n_q == 1:
            step(0)
        else:
            lax.fori_loop(0, n_q, body, 0)

    everything(quick)
    fine = None
    for i in range(n_q):
        total = ml_out[i][1:2, :]
        good = jnp.where((total < TOO_BIG) & (total > TOO_SMALL), 1.0, 0.0)
        fine = good if fine is None else jnp.minimum(fine, good)

    @pl.when(jnp.min(fine) < 0.5)
    def _():
        everything(careful)

    if plan["finish"]:
        for i in range(n_q):
            m, total = ml_out[i][0:1, :], ml_out[i][1:2, :]
            out_refs[i][0:HEAD, :] = (acc_out[i] * (1.0 / total)).astype(jnp.bfloat16)
            out_refs[i][HEAD:, :] = coded_mass(m + jnp.log2(total))


def coded_mass(mass):
    a = mass.astype(jnp.bfloat16).astype(jnp.float32)
    b = (mass - a).astype(jnp.bfloat16).astype(jnp.float32)
    c = mass - a - b
    rows = lax.broadcasted_iota(jnp.int32, (META, ROWS), 0)
    return jnp.where(rows == 0, a, jnp.where(rows == 1, b, jnp.where(rows == 2, c, 0.0))).astype(jnp.bfloat16)


def attend(name, queries, kvs, state=None, fresh=(), finish=False, skip=0):
    n_q = len(queries)
    plan = dict(
        n_q=n_q,
        n_kv=len(kvs),
        n_fresh=len(fresh),
        start=state is None,
        finish=finish,
        skip=skip,
    )
    acc = jax.ShapeDtypeStruct((n_q, HEAD, ROWS), jnp.float32)
    ml = jax.ShapeDtypeStruct((n_q, 8, ROWS), jnp.float32)
    scratch = [pltpu.VMEM((n_q, HEAD + META, ROWS), jnp.bfloat16)]
    if fresh:
        scratch += [
            pltpu.VMEM((2 * len(fresh) * TOK, HEAD), jnp.bfloat16),
            pltpu.VMEM((len(fresh) * TOK, TOK), jnp.float32),
        ]
    if finish:
        outs = [jax.ShapeDtypeStruct((HEAD + META, ROWS), jnp.bfloat16)] * n_q
        scratch += [pltpu.VMEM(acc.shape, jnp.float32), pltpu.VMEM(ml.shape, jnp.float32)]
    else:
        outs = [acc, ml]
    args = list(queries) + list(kvs) + list(fresh) + list(state or ())
    pairs = n_q * (len(kvs) * CHUNK + len(fresh) * TOK) * ROWS
    return pl.pallas_call(
        functools.partial(attend_kernel, plan),
        out_shape=outs,
        in_specs=[VMEM] * len(args),
        out_specs=[VMEM] * len(outs),
        scratch_shapes=scratch,
        compiler_params=pltpu.CompilerParams(vmem_limit_bytes=24 * 2**20),
        cost_estimate=pl.CostEstimate(flops=pairs * 1024, bytes_accessed=0, transcendentals=0),
        name=name,
    )(*args)


def combine_kernel(acc_ref, ml_ref, *refs):
    parts, (att_ref, mass_ref) = refs[:-2], refs[-2:]
    total = ml_ref[0][1:2, :]
    masses = [ml_ref[0][0:1, :] + jnp.log2(total)]
    for r in parts:
        rows = r[HEAD:, :].astype(jnp.float32)
        masses.append(rows[0:1, :] + rows[1:2, :] + rows[2:3, :])
    top = functools.reduce(jnp.maximum, masses)
    weights = [jnp.exp2(m - top) for m in masses]
    den = functools.reduce(jnp.add, weights)
    mass = (top + jnp.log2(den)) * LN2
    shares = [w / den for w in weights]
    shares[0] = shares[0] / total
    for g in range(GROUP):
        lanes = slice(g * TOK, (g + 1) * TOK)
        x = acc_ref[0, :, lanes] * shares[0][:, lanes]
        for r, w in zip(parts, shares[1:]):
            x = x + r[0:HEAD, lanes].astype(jnp.float32) * w[:, lanes]
        att_ref[:, lanes] = x.T.astype(jnp.bfloat16)
    mass_ref[...] = jnp.concatenate([mass[:, g * TOK : (g + 1) * TOK] for g in range(GROUP)], 0)


def prepare(name, kernel, shape, args, specs, work, dtype=jnp.bfloat16):
    return pl.pallas_call(
        kernel,
        out_shape=jax.ShapeDtypeStruct(shape, dtype),
        in_specs=specs,
        out_specs=VMEM,
        compiler_params=pltpu.CompilerParams(vmem_limit_bytes=8 * 2**20),
        cost_estimate=pl.CostEstimate(flops=work, bytes_accessed=0, transcendentals=0),
        name=name,
    )(*args)


def per_device(queries, k, v, fk, fv, positions, order, span):
    order = order.reshape(1, TOK)
    positions = positions.reshape(2 * CHUNK // TOK, TOK)
    angle = prepare("angles", angle_kernel, (HEAD + META, TOK), (order,), [VMEM], 10**9, jnp.float32)
    q0 = prepare("turn_queries", query_kernel, (HEAD + META, ROWS), (queries, angle), [VMEM] * 2, 10**9)
    q_near = [shift(q0, "queries", -1), shift(q0, "queries", 1)]
    q_far = shift(q0, "queries", 2)

    first = prepare(
        "turn_keys_first",
        functools.partial(key_kernel, 0),
        (2 * CHUNK, HEAD),
        (k, v, positions),
        [VMEM] * 3,
        2 * 10**9,
    )
    first_near = [shift(first, "keys", -1), shift(first, "keys", 1)]
    second = prepare(
        "turn_keys_second",
        functools.partial(key_kernel, CHUNK),
        (PLACES + META, HEAD),
        (k, v, positions, fk, fv, order, span),
        [VMEM] * 6 + [pl.BlockSpec(memory_space=pltpu.SMEM)],
        2 * 10**9,
    )
    second_near = [shift(second, "keys", -1), shift(second, "keys", 1)]

    mine = attend("mine_own", [q0], [first, second])
    state = attend("others_own", [q_far, *q_near], [first, second])
    far = attend("far_first", [q_far], first_near, state)
    far, state, behind, ahead = lax.optimization_barrier((far, state, first_near[1], second_near[0]))
    first_far = shift(behind, "keys", 1)
    second_far = shift(ahead, "keys", -1)
    near = attend("near_near", q_near, [*first_near, *second_near], state, skip=1)
    fresh = [second, *second_near, second_far]
    r_ahead, r_behind = attend("near_last", q_near, [first_far, second_far], near, fresh, finish=True)
    (r_far,) = attend("far_last", [q_far], [*second_near, first_far, second_far], far, fresh, finish=True)
    back = [shift(r_far, "queries", 2), shift(r_ahead, "queries", 1), shift(r_behind, "queries", -1)]
    mine = attend("mine_rest", [q0], [*first_near, *second_near, first_far, second_far], mine, fresh)
    attended, mass = pl.pallas_call(
        combine_kernel,
        out_shape=[
            jax.ShapeDtypeStruct((TOK, GROUP * HEAD), jnp.bfloat16),
            jax.ShapeDtypeStruct((GROUP, TOK), jnp.float32),
        ],
        in_specs=[VMEM] * 5,
        out_specs=[VMEM] * 2,
        compiler_params=pltpu.CompilerParams(vmem_limit_bytes=8 * 2**20),
        name="combine",
    )(*mine, *back)
    return attended, mass.T


def solution(mesh):
    spec = (P("ctx", "tp"),) * 5 + (P("ctx"),) * 3
    return jax.shard_map(
        per_device,
        mesh=mesh,
        in_specs=spec,
        out_specs=(P("ctx", "tp"), P("ctx", "tp")),
        check_vma=False,
    )
```

profile of v0, /device:TPU:0, one launch (start us, length us, event | category | flops | bytes accessed | tf_op | source)
XLA Modules:
  0.0 449.2 jit_solution(3958320680875391436)
XLA Ops:
  0.6 0.0 copy-start.6
  0.6 0.6 copy-done.6
  1.3 0.0 copy-start.2
  1.3 0.1 angles.1.angle_ref
  1.4 0.9 copy-done.2
  2.2 0.0 copy-start
  2.2 0.0 copy-start.1
  2.2 0.0 copy-start.5
  2.2 0.2 turn_queries.1.refs_0_
  2.4 4.0 collective-permute-start.4
  6.5 0.7 collective-permute-start.5
  7.2 1.3 collective-permute-start.6
  8.5 0.0 copy-done
  8.5 0.0 copy-done.1
  8.5 0.0 copy-done.5
  8.5 0.0 copy-start.3
  8.5 0.0 copy-start.4
  8.5 0.0 copy-start.7
  8.5 0.7 turn_keys_first.1.refs_3_.refs_1_
  9.2 1.6 collective-permute-start.1
  10.8 1.7 collective-permute-start
  13.1 0.0 copy-done.3
  13.1 0.0 copy-done.4
  13.2 0.0 copy-done.7
  13.2 0.7 turn_keys_second.1.refs_4_.refs_2_.refs_7_.refs_5_
  13.9 25.0 %mine_own.1 = (f32[1,128,1024]{2,1,0:T(8,128)S(1)}, f32[1,8,1024]{2,1,0:T(8,128)S(1)}) custom-call(bf16[144,1024]{1,0:T(8,128)(2,1)S(1)} %turn_queries.1.refs_0_, bf16[2048,128]{1,0:T(8,128)(2,1)S(1)} %turn_keys_first.1.refs_3_.refs_1_, bf16[2320,128]{1,0:T(8,128)(2,1)S(1)} %turn_keys_second.1.refs_4_.refs_2_.refs_7_.refs_5_), custom_call_target="tpu_custom_call" | custom-call | flops 2147483648 | tf_op jit(solution)/shard_map/mine_own/pallas_call | solution.py:352
  38.9 0.0 collective-permute-done.4.refs_0_
  38.9 1.9 collective-permute-start.2
  40.8 0.0 collective-permute-done.5.refs_1_.refs_0_
  40.8 0.2 collective-permute-start.3
  41.0 0.0 collective-permute-done.6.refs_2_.refs_1_
  41.0 75.1 %others_own.1 = (f32[3,128,1024]{2,1,0:T(8,128)S(1)}, f32[3,8,1024]{2,1,0:T(8,128)S(1)}) custom-call(bf16[144,1024]{1,0:T(8,128)(2,1)S(1)} %collective-permute-done.4.refs_0_, bf16[144,1024]{1,0:T(8,128)(2,1)S(1)} %collective-permute-done.5.refs_1_.refs_0_, bf16[144,1024]{1,0:T(8,128)(2,1)S(1)} %collective-permute-done.6.refs_2_.refs_1_, ...), custom_call_target="tpu_custom_call" | custom-call | flops 6442450944 | tf_op jit(solution)/shard_map/others_own/pallas_call | solution.py:352
  116.1 0.0 collective-permute-done.1.refs_2_.refs_3_
  116.1 0.0 collective-permute-done.refs_1_.refs_2_
  116.1 25.1 %far_first.1 = (f32[1,128,1024]{2,1,0:T(8,128)S(1)}, f32[1,8,1024]{2,1,0:T(8,128)S(1)}) custom-call(bf16[144,1024]{1,0:T(8,128)(2,1)S(1)} %collective-permute-done.4.refs_0_, bf16[2048,128]{1,0:T(8,128)(2,1)S(1)} %collective-permute-done.refs_1_.refs_2_, bf16[2048,128]{1,0:T(8,128)(2,1)S(1)} %collective-permute-done.1.refs_2_.refs_3_, ...), custom_call_target="tpu_custom_call" | custom-call | flops 2147483648 | tf_op jit(solution)/shard_map/far_first/pallas_call | solution.py:352
  141.2 0.0 collective-permute-done.2.refs_3_.refs_8_.refs_1_.refs_6_.refs_4_.refs_5_
  141.2 3.1 collective-permute-start.8
  144.3 0.0 collective-permute-start.7
  144.3 0.0 collective-permute-done.3.refs_4_.refs_9_.refs_2_.refs_7_.refs_5_.refs_6_
  144.3 99.8 %near_near.1 = (f32[2,128,1024]{2,1,0:T(8,128)S(1)}, f32[2,8,1024]{2,1,0:T(8,128)S(1)}) custom-call(bf16[144,1024]{1,0:T(8,128)(2,1)S(1)} %collective-permute-done.5.refs_1_.refs_0_, bf16[144,1024]{1,0:T(8,128)(2,1)S(1)} %collective-permute-done.6.refs_2_.refs_1_, bf16[2048,128]{1,0:T(8,128)(2,1)S(1)} %collective-permute-done.refs_1_.refs_2_, ...), custom_call_target="tpu_custom_call" | custom-call | flops 8589934592 | tf_op jit(solution)/shard_map/near_near/pallas_call | solution.py:352
  244.1 0.0 collective-permute-done.7.refs_5_.refs_3_.refs_2_
  244.1 0.0 collective-permute-done.8.refs_6_.refs_10_.refs_4_.refs_8_.refs_3_.refs_7_
  244.2 63.0 %near_last.1 = (bf16[144,1024]{1,0:T(8,128)(2,1)S(1)}, bf16[144,1024]{1,0:T(8,128)(2,1)S(1)}) custom-call(bf16[144,1024]{1,0:T(8,128)(2,1)S(1)} %collective-permute-done.5.refs_1_.refs_0_, bf16[144,1024]{1,0:T(8,128)(2,1)S(1)} %collective-permute-done.6.refs_2_.refs_1_, bf16[2048,128]{1,0:T(8,128)(2,1)S(1)} %collective-permute-done.7.refs_5_.refs_3_.refs_2_, ...), custom_call_target="tpu_custom_call" | custom-call | flops 5368709120 | tf_op jit(solution)/shard_map/near_last/pallas_call | solution.py:352
  307.2 1.1 collective-permute-start.10
  308.3 2.2 collective-permute-start.11
  310.5 56.5 %far_last.1 = bf16[144,1024]{1,0:T(8,128)(2,1)S(1)} custom-call(bf16[144,1024]{1,0:T(8,128)(2,1)S(1)} %collective-permute-done.4.refs_0_, bf16[2320,128]{1,0:T(8,128)(2,1)S(1)} %collective-permute-done.2.refs_3_.refs_8_.refs_1_.refs_6_.refs_4_.refs_5_, bf16[2320,128]{1,0:T(8,128)(2,1)S(1)} %collective-permute-done.3.refs_4_.refs_9_.refs_2_.refs_7_.refs_5_.refs_6_, ...), custom_call_target="tpu_custom_call" | custom-call | flops 4831838208 | tf_op jit(solution)/shard_map/far_last/pallas_call | solution.py:352
  367.0 0.2 collective-permute-start.9
  367.2 80.9 %mine_rest.1 = (f32[1,128,1024]{2,1,0:T(8,128)S(1)}, f32[1,8,1024]{2,1,0:T(8,128)S(1)}) custom-call(bf16[144,1024]{1,0:T(8,128)(2,1)S(1)} %turn_queries.1.refs_0_, bf16[2048,128]{1,0:T(8,128)(2,1)S(1)} %collective-permute-done.refs_1_.refs_2_, bf16[2048,128]{1,0:T(8,128)(2,1)S(1)} %collective-permute-done.1.refs_2_.refs_3_, ...), custom_call_target="tpu_custom_call" | custom-call | flops 6979321856 | tf_op jit(solution)/shard_map/mine_rest/pallas_call | solution.py:352
  448.1 0.0 collective-permute-done.10.refs_1_
  448.1 0.0 collective-permute-done.11.refs_2_
  448.1 0.0 collective-permute-done.9.refs_0_
  448.1 1.0 combine.1
Async XLA Ops:
  0.6 0.7 copy-start.6
  1.3 0.9 copy-start.2
  2.2 6.2 %copy-start = (bf16[2048,128]{1,0:T(8,128)(2,1)S(1)}, bf16[2048,128]{1,0:T(8,128)(2,1)}, u32[]{:S(2)}) copy-start(bf16[2048,128]{1,0:T(8,128)(2,1)} %k_ref.3) | copy-start | bytes 1572868
  2.2 6.2 %copy-start.1 = (bf16[2048,128]{1,0:T(8,128)(2,1)S(1)}, bf16[2048,128]{1,0:T(8,128)(2,1)}, u32[]{:S(2)}) copy-start(bf16[2048,128]{1,0:T(8,128)(2,1)} %v_ref.3) | copy-start | bytes 1572868
  2.2 6.2 %copy-start.5 = (s32[2048]{0:T(1024)S(1)}, s32[2048]{0:T(1024)}, u32[]{:S(2)}) copy-start(s32[2048]{0:T(1024)} %param.13) | copy-start | bytes 24580
  2.4 36.5 %collective-permute-start.4 = (bf16[144,1024]{1,0:T(8,128)(2,1)S(1)}, bf16[144,1024]{1,0:T(8,128)(2,1)S(1)}, u32[]{:S(2)}, u32[]{:S(2)}) collective-permute-start(bf16[144,1024]{1,0:T(8,128)(2,1)S(1)} %turn_queries.1.refs_0_), channel_id=1, source_target_pairs={{0,64},{1,17},{2,66},{3,19},{4,68},{5,21},{6,70},{7,23},{8,72},{9,... | collective-permute-start | bytes 884744 | tf_op jit(solution)/shard_map/ppermute | solution.py:41
  6.5 34.3 %collective-permute-start.5 = (bf16[144,1024]{1,0:T(8,128)(2,1)S(1)}, bf16[144,1024]{1,0:T(8,128)(2,1)S(1)}, u32[]{:S(2)}, u32[]{:S(2)}) collective-permute-start(bf16[144,1024]{1,0:T(8,128)(2,1)S(1)} %turn_queries.1.refs_0_), channel_id=1, source_target_pairs={{0,96},{1,25},{2,98},{3,27},{4,100},{5,29},{6,102},{7,31},{8,104},... | collective-permute-start | bytes 884744 | tf_op jit(solution)/shard_map/ppermute | solution.py:41
  7.2 33.9 %collective-permute-start.6 = (bf16[144,1024]{1,0:T(8,128)(2,1)S(1)}, bf16[144,1024]{1,0:T(8,128)(2,1)S(1)}, u32[]{:S(2)}, u32[]{:S(2)}) collective-permute-start(bf16[144,1024]{1,0:T(8,128)(2,1)S(1)} %turn_queries.1.refs_0_), channel_id=1, source_target_pairs={{0,32},{1,9},{2,34},{3,11},{4,36},{5,13},{6,38},{7,15},{8,40},{9,1... | collective-permute-start | bytes 884744 | tf_op jit(solution)/shard_map/ppermute | solution.py:41
  8.5 4.6 %copy-start.3 = (bf16[128,128]{1,0:T(8,128)(2,1)S(1)}, bf16[128,128]{1,0:T(8,128)(2,1)}, u32[]{:S(2)}) copy-start(bf16[128,128]{1,0:T(8,128)(2,1)} %refs_0_.1) | copy-start | bytes 98308
  8.5 4.6 %copy-start.4 = (bf16[128,128]{1,0:T(8,128)(2,1)S(1)}, bf16[128,128]{1,0:T(8,128)(2,1)}, u32[]{:S(2)}) copy-start(bf16[128,128]{1,0:T(8,128)(2,1)} %refs_1_.1) | copy-start | bytes 98308
  8.5 4.6 %copy-start.7 = (s32[128]{0:T(128)S(1)}, s32[128]{0:T(128)}, u32[]{:S(2)}) copy-start(s32[128]{0:T(128)} %param.14) | copy-start | bytes 1540
  9.2 106.9 %collective-permute-start.1 = (bf16[2048,128]{1,0:T(8,128)(2,1)S(1)}, bf16[2048,128]{1,0:T(8,128)(2,1)S(1)}, u32[]{:S(2)}, u32[]{:S(2)}) collective-permute-start(bf16[2048,128]{1,0:T(8,128)(2,1)S(1)} %turn_keys_first.1.refs_3_.refs_1_), channel_id=1, source_target_pairs={{0,8},{1,33},{2,10},{3,35},{4,12},{5,37},{6,14},{7,39},{8,16},{9,4... | collective-permute-start | bytes 1572872 | tf_op jit(solution)/shard_map/ppermute | solution.py:41
  10.8 105.3 %collective-permute-start = (bf16[2048,128]{1,0:T(8,128)(2,1)S(1)}, bf16[2048,128]{1,0:T(8,128)(2,1)S(1)}, u32[]{:S(2)}, u32[]{:S(2)}) collective-permute-start(bf16[2048,128]{1,0:T(8,128)(2,1)S(1)} %turn_keys_first.1.refs_3_.refs_1_), channel_id=1, source_target_pairs={{0,24},{1,97},{2,26},{3,99},{4,28},{5,101},{6,30},{7,103},{8,0},{9... | collective-permute-start | bytes 1572872 | tf_op jit(solution)/shard_map/ppermute | solution.py:41
  38.9 102.3 %collective-permute-start.2 = (bf16[2320,128]{1,0:T(8,128)(2,1)S(1)}, bf16[2320,128]{1,0:T(8,128)(2,1)S(1)}, u32[]{:S(2)}, u32[]{:S(2)}) collective-permute-start(bf16[2320,128]{1,0:T(8,128)(2,1)S(1)} %turn_keys_second.1.refs_4_.refs_2_.refs_7_.refs_5_), channel_id=1, source_target_pairs={{0,24},{1,97},{2,26},{3,99},{4,28},{5,101},{6,30},{7,103},{8,0},{9... | collective-permute-start | bytes 1781768 | tf_op jit(solution)/shard_map/ppermute | solution.py:41
  40.8 103.5 %collective-permute-start.3 = (bf16[2320,128]{1,0:T(8,128)(2,1)S(1)}, bf16[2320,128]{1,0:T(8,128)(2,1)S(1)}, u32[]{:S(2)}, u32[]{:S(2)}) collective-permute-start(bf16[2320,128]{1,0:T(8,128)(2,1)S(1)} %turn_keys_second.1.refs_4_.refs_2_.refs_7_.refs_5_), channel_id=1, source_target_pairs={{0,8},{1,33},{2,10},{3,35},{4,12},{5,37},{6,14},{7,39},{8,16},{9,4... | collective-permute-start | bytes 1781768 | tf_op jit(solution)/shard_map/ppermute | solution.py:41
  141.2 102.9 %collective-permute-start.8 = (bf16[2320,128]{1,0:T(8,128)(2,1)S(1)}, bf16[2320,128]{1,0:T(8,128)(2,1)S(1)}, u32[]{:S(2)}, u32[]{:S(2)}) collective-permute-start(bf16[2320,128]{1,0:T(8,128)(2,1)S(1)} %collective-permute-done.2.refs_3_.refs_8_.refs_1_.refs_6_.refs_4_.refs_5_), channel_id=1, source_target_pairs={{0,24},{1,97},{2,26},{3,99},{4,28},{5,101},{6,30},{7,103},{8,0},{9... | collective-permute-start | bytes 1781768 | tf_op jit(solution)/shard_map/ppermute | solution.py:41
  144.3 99.8 %collective-permute-start.7 = (bf16[2048,128]{1,0:T(8,128)(2,1)S(1)}, bf16[2048,128]{1,0:T(8,128)(2,1)S(1)}, u32[]{:S(2)}, u32[]{:S(2)}) collective-permute-start(bf16[2048,128]{1,0:T(8,128)(2,1)S(1)} %collective-permute-done.1.refs_2_.refs_3_), channel_id=1, source_target_pairs={{0,8},{1,33},{2,10},{3,35},{4,12},{5,37},{6,14},{7,39},{8,16},{9,4... | collective-permute-start | bytes 1572872 | tf_op jit(solution)/shard_map/ppermute | solution.py:41
  307.2 140.9 %collective-permute-start.10 = (bf16[144,1024]{1,0:T(8,128)(2,1)S(1)}, bf16[144,1024]{1,0:T(8,128)(2,1)S(1)}, u32[]{:S(2)}, u32[]{:S(2)}) collective-permute-start(bf16[144,1024]{1,0:T(8,128)(2,1)S(1)} %get-tuple-element.38), channel_id=1, source_target_pairs={{0,32},{1,9},{2,34},{3,11},{4,36},{5,13},{6,38},{7,15},{8,40},{9,1... | collective-permute-start | bytes 884744 | tf_op jit(solution)/shard_map/ppermute | solution.py:41
  308.3 139.8 %collective-permute-start.11 = (bf16[144,1024]{1,0:T(8,128)(2,1)S(1)}, bf16[144,1024]{1,0:T(8,128)(2,1)S(1)}, u32[]{:S(2)}, u32[]{:S(2)}) collective-permute-start(bf16[144,1024]{1,0:T(8,128)(2,1)S(1)} %get-tuple-element.39), channel_id=1, source_target_pairs={{0,96},{1,25},{2,98},{3,27},{4,100},{5,29},{6,102},{7,31},{8,104},... | collective-permute-start | bytes 884744 | tf_op jit(solution)/shard_map/ppermute | solution.py:41
  367.0 81.2 %collective-permute-start.9 = (bf16[144,1024]{1,0:T(8,128)(2,1)S(1)}, bf16[144,1024]{1,0:T(8,128)(2,1)S(1)}, u32[]{:S(2)}, u32[]{:S(2)}) collective-permute-start(bf16[144,1024]{1,0:T(8,128)(2,1)S(1)} %far_last.1), channel_id=1, source_target_pairs={{0,64},{1,17},{2,66},{3,19},{4,68},{5,21},{6,70},{7,23},{8,72},{9,... | collective-permute-start | bytes 884744 | tf_op jit(solution)/shard_map/ppermute | solution.py:41
where the time goes:
time: 449 us
  Pallas kernels  428 us (95%)
  starting transfers between devices  18.1 us (4%)
    pallas_call x7, Pallas kernels, attend(): pl.pallas_call(functools.partial(attend_kernel, plan), out_shape=outs, in...  425 us
    ppermute x12, starting transfers between devices, shift(): return lax.ppermute(block, ('ctx', 'tp'), pairs)  18.1 us
  transfers between devices with their start and end apart: 12, of which 0 were waited for; matrix products, arithmetic and copies ran while one was open for 0% of the time, Pallas kernels for 81%

commit v1 on v0

--- a/solution.py
+++ b/solution.py
@@ -18,7 +18,7 @@
 CHUNK = 1024
 TP = 8
 KT = 256
-LOG2E = 1.4426950408889634
+SCALE = HEAD**-0.5 * 1.4426950408889634
 LN2 = 0.6931471805599453
 LOW = -1e30
 TOO_BIG = 2.0**100
@@ -115,9 +115,8 @@
     order = order_ref[...]
     turns = [spread(piece) for piece in TURNS]
     cos, sin = angles((order + CACHED).astype(jnp.float32), turns)
-    scale = HEAD**-0.5 * LOG2E
-    out_ref[0:64, :] = cos * scale
-    out_ref[64:128, :] = sin * scale
+    out_ref[0:64, :] = cos
+    out_ref[64:128, :] = sin
     out_ref[128:, :] = coded(order).astype(jnp.float32)
 
 
@@ -202,7 +201,7 @@
         return jnp.concatenate([ref[pl.ds(aligned(first + j * TOK), TOK), :] for j in range(KT // TOK)], 1)
 
     def scores(ref, first, item, masked):
-        s = dot(k_tile(ref, first), q_s[item, 0:HEAD, :])
+        s = dot(k_tile(ref, first), q_s[item, 0:HEAD, :]) * SCALE
         if masked:
             mine = places_of(q_s[item, HEAD:, 0:TOK])
             mask = place_s[pl.ds(aligned(first), KT), :] <= mine
@@ -228,10 +227,7 @@
     def quick(item):
         tiles = [(ref, first, values, masked) for ref, values, n, masked in sources for first in range(0, n, KT)]
         old = old_of(item)
-        if old is None:
-            m, total, acc = None, None, None
-        else:
-            m, total, acc = old
+        total, acc = (None, None) if old is None else old[1:]
         part = jnp.zeros((8, ROWS), jnp.float32)
 
         def scores_of(tile):
@@ -242,16 +238,12 @@
             s = ahead
             if j + 1 < len(tiles):
                 ahead = scores_of(tiles[j + 1])
-            p = jnp.exp2(s) if m is None else jnp.exp2(s - m)
+            p = jnp.exp2(s)
             part = part + jnp.sum(p.reshape(KT // 8, 8, ROWS), 0)
             pv = dot(v_tile(ref, values + first), p.astype(jnp.bfloat16))
             acc = pv if acc is None else acc + pv
         part = jnp.sum(part, 0, keepdims=True)
-        if m is None:
-            m, total = jnp.zeros((1, ROWS), jnp.float32), part
-        else:
-            total = total + part
-        put(item, m, total, acc)
+        put(item, jnp.zeros((1, ROWS), jnp.float32), part if total is None else total + part, acc)
 
     def careful(item):
         def group(g, carry):
@@ -269,7 +261,7 @@
                 def step(t, state, ref=ref, values=values, masked=masked):
                     m, total, acc = state
                     first = t * KT
-                    s = dot(k_tile(ref, first), q)
+                    s = dot(k_tile(ref, first), q) * SCALE
                     if masked:
                         mine = places_of(q_s[item, HEAD:, 0:TOK])
                         s = jnp.where(place_s[pl.ds(aligned(first), KT), :] <= mine, s, LOW)
@@ -303,6 +295,8 @@
     for i in range(n_q):
         total = ml_out[i][1:2, :]
         good = jnp.where((total < TOO_BIG) & (total > TOO_SMALL), 1.0, 0.0)
+        if not plan["start"]:
+            good = jnp.where(ml_in[i + skip][0:1, :] == 0.0, good, 0.0)
         fine = good if fine is None else jnp.minimum(fine, good)
 
     @pl.when(jnp.min(fine) < 0.5)
@@ -429,9 +423,11 @@
     first_far = shift(behind, "keys", 1)
     second_far = shift(ahead, "keys", -1)
     near = attend("near_near", q_near, [*first_near, *second_near], state, skip=1)
+    far = attend("far_second", [q_far], second_near, far)
+    near, far = lax.optimization_barrier((near, far))
     fresh = [second, *second_near, second_far]
     r_ahead, r_behind = attend("near_last", q_near, [first_far, second_far], near, fresh, finish=True)
-    (r_far,) = attend("far_last", [q_far], [*second_near, first_far, second_far], far, fresh, finish=True)
+    (r_far,) = attend("far_last", [q_far], [first_far, second_far], far, fresh, finish=True)
     back = [shift(r_far, "queries", 2), shift(r_ahead, "queries", 1), shift(r_behind, "queries", -1)]
     mine = attend("mine_rest", [q0], [*first_near, *second_near, first_far, second_far], mine, fresh)
     attended, mass = pl.pallas_call(

time: 449 us -> 452 us (level)
    pallas_call x7 -> x8, Pallas kernels: 425 us -> 428 us  [attend(): pl.pallas_call(functools.partial(attend_kernel, plan), out_shape=outs, in...]
where the time goes in v1:
time: 452 us; the launch traced here: 451 us
  Pallas kernels  430 us (95%)
  starting transfers between devices  18.1 us (4%)
    pallas_call x8, Pallas kernels, attend(): pl.pallas_call(functools.partial(attend_kernel, plan), out_shape=outs, in...  428 us
    ppermute x12, starting transfers between devices, shift(): return lax.ppermute(block, ('ctx', 'tp'), pairs)  18.1 us
  transfers between devices with their start and end apart: 12, of which 0 were waited for; matrix products, arithmetic and copies ran while one was open for 0% of the time, Pallas kernels for 81%

profile of v1, /device:TPU:0, one launch (start us, length us, event | category | flops | bytes accessed | tf_op | source)
XLA Modules:
  0.0 451.5 jit_solution(14615505140997463181)
XLA Ops:
  0.6 0.0 copy-start.6
  0.6 0.6 copy-done.6
  1.3 0.0 copy-start.2
  1.3 0.1 angles.1.angle_ref
  1.4 0.9 copy-done.2
  2.2 0.0 copy-start
  2.2 0.0 copy-start.1
  2.2 0.0 copy-start.5
  2.2 0.2 turn_queries.1.refs_0_
  2.4 4.0 collective-permute-start.4
  6.5 0.7 collective-permute-start.5
  7.2 1.3 collective-permute-start.6
  8.5 0.0 copy-done
  8.5 0.0 copy-done.1
  8.5 0.0 copy-done.5
  8.5 0.0 copy-start.3
  8.5 0.0 copy-start.4
  8.5 0.0 copy-start.7
  8.5 0.7 turn_keys_first.1.refs_3_.refs_1_
  9.2 1.6 collective-permute-start.1
  10.8 1.7 collective-permute-start
  13.1 0.0 copy-done.3
  13.1 0.0 copy-done.4
  13.2 0.0 copy-done.7
  13.2 0.7 turn_keys_second.1.refs_4_.refs_2_.refs_7_.refs_3_
  13.9 25.2 %mine_own.1 = (f32[1,128,1024]{2,1,0:T(8,128)S(1)}, f32[1,8,1024]{2,1,0:T(8,128)S(1)}) custom-call(bf16[144,1024]{1,0:T(8,128)(2,1)S(1)} %turn_queries.1.refs_0_, bf16[2048,128]{1,0:T(8,128)(2,1)S(1)} %turn_keys_first.1.refs_3_.refs_1_, bf16[2320,128]{1,0:T(8,128)(2,1)S(1)} %turn_keys_second.1.refs_4_.refs_2_.refs_7_.refs_3_), custom_call_target="tpu_custom_call" | custom-call | flops 2147483648 | tf_op jit(solution)/shard_map/mine_own/pallas_call | solution.py:346
  39.1 0.0 collective-permute-done.4.refs_0_
  39.1 1.9 collective-permute-start.2
  41.0 0.0 collective-permute-done.5.refs_1_.refs_0_
  41.0 0.2 collective-permute-start.3
  41.2 0.0 collective-permute-done.6.refs_2_.refs_1_
  41.2 75.5 %others_own.1 = (f32[3,128,1024]{2,1,0:T(8,128)S(1)}, f32[3,8,1024]{2,1,0:T(8,128)S(1)}) custom-call(bf16[144,1024]{1,0:T(8,128)(2,1)S(1)} %collective-permute-done.4.refs_0_, bf16[144,1024]{1,0:T(8,128)(2,1)S(1)} %collective-permute-done.5.refs_1_.refs_0_, bf16[144,1024]{1,0:T(8,128)(2,1)S(1)} %collective-permute-done.6.refs_2_.refs_1_, ...), custom_call_target="tpu_custom_call" | custom-call | flops 6442450944 | tf_op jit(solution)/shard_map/others_own/pallas_call | solution.py:346
  116.7 0.0 collective-permute-done.1.refs_2_.refs_3_
  116.7 0.0 collective-permute-done.refs_1_.refs_2_
  116.7 25.2 %far_first.1 = (f32[1,128,1024]{2,1,0:T(8,128)S(1)}, f32[1,8,1024]{2,1,0:T(8,128)S(1)}) custom-call(bf16[144,1024]{1,0:T(8,128)(2,1)S(1)} %collective-permute-done.4.refs_0_, bf16[2048,128]{1,0:T(8,128)(2,1)S(1)} %collective-permute-done.refs_1_.refs_2_, bf16[2048,128]{1,0:T(8,128)(2,1)S(1)} %collective-permute-done.1.refs_2_.refs_3_, ...), custom_call_target="tpu_custom_call" | custom-call | flops 2147483648 | tf_op jit(solution)/shard_map/far_first/pallas_call | solution.py:346
  142.0 0.0 collective-permute-done.2.refs_3_.refs_8_.refs_4_.refs_1_.refs_5_
  142.0 3.1 collective-permute-start.8
  145.0 0.0 collective-permute-start.7
  145.0 0.0 collective-permute-done.3.refs_4_.refs_9_.refs_5_.refs_2_.refs_6_
  145.0 25.3 %far_second.1 = (f32[1,128,1024]{2,1,0:T(8,128)S(1)}, f32[1,8,1024]{2,1,0:T(8,128)S(1)}) custom-call(bf16[144,1024]{1,0:T(8,128)(2,1)S(1)} %collective-permute-done.4.refs_0_, bf16[2320,128]{1,0:T(8,128)(2,1)S(1)} %collective-permute-done.2.refs_3_.refs_8_.refs_4_.refs_1_.refs_5_, ...), custom_call_target="tpu_custom_call" | custom-call | flops 2147483648 | tf_op jit(solution)/shard_map/far_second/pallas_call | solution.py:346
  170.4 100.2 %near_near.1 = (f32[2,128,1024]{2,1,0:T(8,128)S(1)}, f32[2,8,1024]{2,1,0:T(8,128)S(1)}) custom-call(bf16[144,1024]{1,0:T(8,128)(2,1)S(1)} %collective-permute-done.5.refs_1_.refs_0_, bf16[144,1024]{1,0:T(8,128)(2,1)S(1)} %collective-permute-done.6.refs_2_.refs_1_, bf16[2048,128]{1,0:T(8,128)(2,1)S(1)} %collective-permute-done.refs_1_.refs_2_, ...), custom_call_target="tpu_custom_call" | custom-call | flops 8589934592 | tf_op jit(solution)/shard_map/near_near/pallas_call | solution.py:346
  270.6 0.0 collective-permute-done.7.refs_5_.refs_1_.refs_2_
  270.6 0.0 collective-permute-done.8.refs_6_.refs_10_.refs_2_.refs_3_.refs_7_
  270.6 63.2 %near_last.1 = (bf16[144,1024]{1,0:T(8,128)(2,1)S(1)}, bf16[144,1024]{1,0:T(8,128)(2,1)S(1)}) custom-call(bf16[144,1024]{1,0:T(8,128)(2,1)S(1)} %collective-permute-done.5.refs_1_.refs_0_, bf16[144,1024]{1,0:T(8,128)(2,1)S(1)} %collective-permute-done.6.refs_2_.refs_1_, bf16[2048,128]{1,0:T(8,128)(2,1)S(1)} %collective-permute-done.7.refs_5_.refs_1_.refs_2_, ...), custom_call_target="tpu_custom_call" | custom-call | flops 5368709120 | tf_op jit(solution)/shard_map/near_last/pallas_call | solution.py:346
  333.8 1.1 collective-permute-start.10
  334.9 2.2 collective-permute-start.11
  337.1 31.6 %far_last.1 = bf16[144,1024]{1,0:T(8,128)(2,1)S(1)} custom-call(bf16[144,1024]{1,0:T(8,128)(2,1)S(1)} %collective-permute-done.4.refs_0_, bf16[2048,128]{1,0:T(8,128)(2,1)S(1)} %collective-permute-done.7.refs_5_.refs_1_.refs_2_, bf16[2320,128]{1,0:T(8,128)(2,1)S(1)} %collective-permute-done.8.refs_6_.refs_10_.refs_2_.refs_3_.refs_7_, ...), custom_call_target="tpu_custom_call" | custom-call | flops 2684354560 | tf_op jit(solution)/shard_map/far_last/pallas_call | solution.py:346
  368.7 0.2 collective-permute-start.9
  368.9 81.5 %mine_rest.1 = (f32[1,128,1024]{2,1,0:T(8,128)S(1)}, f32[1,8,1024]{2,1,0:T(8,128)S(1)}) custom-call(bf16[144,1024]{1,0:T(8,128)(2,1)S(1)} %turn_queries.1.refs_0_, bf16[2048,128]{1,0:T(8,128)(2,1)S(1)} %collective-permute-done.refs_1_.refs_2_, bf16[2048,128]{1,0:T(8,128)(2,1)S(1)} %collective-permute-done.1.refs_2_.refs_3_, ...), custom_call_target="tpu_custom_call" | custom-call | flops 6979321856 | tf_op jit(solution)/shard_map/mine_rest/pallas_call | solution.py:346
  450.4 0.0 collective-permute-done.10.refs_1_
  450.4 0.0 collective-permute-done.11.refs_2_
  450.5 0.0 collective-permute-done.9.refs_0_
  450.5 1.0 combine.1
Async XLA Ops:
  0.6 0.7 copy-start.6
  1.3 0.9 copy-start.2
  2.2 6.2 %copy-start = (bf16[2048,128]{1,0:T(8,128)(2,1)S(1)}, bf16[2048,128]{1,0:T(8,128)(2,1)}, u32[]{:S(2)}) copy-start(bf16[2048,128]{1,0:T(8,128)(2,1)} %k_ref.3) | copy-start | bytes 1572868
  2.2 6.2 %copy-start.1 = (bf16[2048,128]{1,0:T(8,128)(2,1)S(1)}, bf16[2048,128]{1,0:T(8,128)(2,1)}, u32[]{:S(2)}) copy-start(bf16[2048,128]{1,0:T(8,128)(2,1)} %v_ref.3) | copy-start | bytes 1572868
  2.2 6.2 %copy-start.5 = (s32[2048]{0:T(1024)S(1)}, s32[2048]{0:T(1024)}, u32[]{:S(2)}) copy-start(s32[2048]{0:T(1024)} %param.13) | copy-start | bytes 24580
  2.4 36.7 %collective-permute-start.4 = (bf16[144,1024]{1,0:T(8,128)(2,1)S(1)}, bf16[144,1024]{1,0:T(8,128)(2,1)S(1)}, u32[]{:S(2)}, u32[]{:S(2)}) collective-permute-start(bf16[144,1024]{1,0:T(8,128)(2,1)S(1)} %turn_queries.1.refs_0_), channel_id=1, source_target_pairs={{0,64},{1,17},{2,66},{3,19},{4,68},{5,21},{6,70},{7,23},{8,72},{9,... | collective-permute-start | bytes 884744 | tf_op jit(solution)/shard_map/ppermute | solution.py:41
  6.5 34.5 %collective-permute-start.5 = (bf16[144,1024]{1,0:T(8,128)(2,1)S(1)}, bf16[144,1024]{1,0:T(8,128)(2,1)S(1)}, u32[]{:S(2)}, u32[]{:S(2)}) collective-permute-start(bf16[144,1024]{1,0:T(8,128)(2,1)S(1)} %turn_queries.1.refs_0_), channel_id=1, source_target_pairs={{0,96},{1,25},{2,98},{3,27},{4,100},{5,29},{6,102},{7,31},{8,104},... | collective-permute-start | bytes 884744 | tf_op jit(solution)/shard_map/ppermute | solution.py:41
  7.2 34.0 %collective-permute-start.6 = (bf16[144,1024]{1,0:T(8,128)(2,1)S(1)}, bf16[144,1024]{1,0:T(8,128)(2,1)S(1)}, u32[]{:S(2)}, u32[]{:S(2)}) collective-permute-start(bf16[144,1024]{1,0:T(8,128)(2,1)S(1)} %turn_queries.1.refs_0_), channel_id=1, source_target_pairs={{0,32},{1,9},{2,34},{3,11},{4,36},{5,13},{6,38},{7,15},{8,40},{9,1... | collective-permute-start | bytes 884744 | tf_op jit(solution)/shard_map/ppermute | solution.py:41
  8.5 4.6 %copy-start.3 = (bf16[128,128]{1,0:T(8,128)(2,1)S(1)}, bf16[128,128]{1,0:T(8,128)(2,1)}, u32[]{:S(2)}) copy-start(bf16[128,128]{1,0:T(8,128)(2,1)} %refs_0_.1) | copy-start | bytes 98308
  8.5 4.6 %copy-start.4 = (bf16[128,128]{1,0:T(8,128)(2,1)S(1)}, bf16[128,128]{1,0:T(8,128)(2,1)}, u32[]{:S(2)}) copy-start(bf16[128,128]{1,0:T(8,128)(2,1)} %refs_1_.1) | copy-start | bytes 98308
  8.5 4.6 %copy-start.7 = (s32[128]{0:T(128)S(1)}, s32[128]{0:T(128)}, u32[]{:S(2)}) copy-start(s32[128]{0:T(128)} %param.14) | copy-start | bytes 1540
  9.2 107.5 %collective-permute-start.1 = (bf16[2048,128]{1,0:T(8,128)(2,1)S(1)}, bf16[2048,128]{1,0:T(8,128)(2,1)S(1)}, u32[]{:S(2)}, u32[]{:S(2)}) collective-permute-start(bf16[2048,128]{1,0:T(8,128)(2,1)S(1)} %turn_keys_first.1.refs_3_.refs_1_), channel_id=1, source_target_pairs={{0,8},{1,33},{2,10},{3,35},{4,12},{5,37},{6,14},{7,39},{8,16},{9,4... | collective-permute-start | bytes 1572872 | tf_op jit(solution)/shard_map/ppermute | solution.py:41
  10.8 105.9 %collective-permute-start = (bf16[2048,128]{1,0:T(8,128)(2,1)S(1)}, bf16[2048,128]{1,0:T(8,128)(2,1)S(1)}, u32[]{:S(2)}, u32[]{:S(2)}) collective-permute-start(bf16[2048,128]{1,0:T(8,128)(2,1)S(1)} %turn_keys_first.1.refs_3_.refs_1_), channel_id=1, source_target_pairs={{0,24},{1,97},{2,26},{3,99},{4,28},{5,101},{6,30},{7,103},{8,0},{9... | collective-permute-start | bytes 1572872 | tf_op jit(solution)/shard_map/ppermute | solution.py:41
  39.1 102.8 %collective-permute-start.2 = (bf16[2320,128]{1,0:T(8,128)(2,1)S(1)}, bf16[2320,128]{1,0:T(8,128)(2,1)S(1)}, u32[]{:S(2)}, u32[]{:S(2)}) collective-permute-start(bf16[2320,128]{1,0:T(8,128)(2,1)S(1)} %turn_keys_second.1.refs_4_.refs_2_.refs_7_.refs_3_), channel_id=1, source_target_pairs={{0,24},{1,97},{2,26},{3,99},{4,28},{5,101},{6,30},{7,103},{8,0},{9... | collective-permute-start | bytes 1781768 | tf_op jit(solution)/shard_map/ppermute | solution.py:41
  41.0 104.1 %collective-permute-start.3 = (bf16[2320,128]{1,0:T(8,128)(2,1)S(1)}, bf16[2320,128]{1,0:T(8,128)(2,1)S(1)}, u32[]{:S(2)}, u32[]{:S(2)}) collective-permute-start(bf16[2320,128]{1,0:T(8,128)(2,1)S(1)} %turn_keys_second.1.refs_4_.refs_2_.refs_7_.refs_3_), channel_id=1, source_target_pairs={{0,8},{1,33},{2,10},{3,35},{4,12},{5,37},{6,14},{7,39},{8,16},{9,4... | collective-permute-start | bytes 1781768 | tf_op jit(solution)/shard_map/ppermute | solution.py:41
  142.0 128.6 %collective-permute-start.8 = (bf16[2320,128]{1,0:T(8,128)(2,1)S(1)}, bf16[2320,128]{1,0:T(8,128)(2,1)S(1)}, u32[]{:S(2)}, u32[]{:S(2)}) collective-permute-start(bf16[2320,128]{1,0:T(8,128)(2,1)S(1)} %collective-permute-done.2.refs_3_.refs_8_.refs_4_.refs_1_.refs_5_), channel_id=1, source_target_pairs={{0,24},{1,97},{2,26},{3,99},{4,28},{5,101},{6,30},{7,103},{8,0},{9... | collective-permute-start | bytes 1781768 | tf_op jit(solution)/shard_map/ppermute | solution.py:41
  145.0 125.5 %collective-permute-start.7 = (bf16[2048,128]{1,0:T(8,128)(2,1)S(1)}, bf16[2048,128]{1,0:T(8,128)(2,1)S(1)}, u32[]{:S(2)}, u32[]{:S(2)}) collective-permute-start(bf16[2048,128]{1,0:T(8,128)(2,1)S(1)} %collective-permute-done.1.refs_2_.refs_3_), channel_id=1, source_target_pairs={{0,8},{1,33},{2,10},{3,35},{4,12},{5,37},{6,14},{7,39},{8,16},{9,4... | collective-permute-start | bytes 1572872 | tf_op jit(solution)/shard_map/ppermute | solution.py:41
  333.8 116.6 %collective-permute-start.10 = (bf16[144,1024]{1,0:T(8,128)(2,1)S(1)}, bf16[144,1024]{1,0:T(8,128)(2,1)S(1)}, u32[]{:S(2)}, u32[]{:S(2)}) collective-permute-start(bf16[144,1024]{1,0:T(8,128)(2,1)S(1)} %get-tuple-element.50), channel_id=1, source_target_pairs={{0,32},{1,9},{2,34},{3,11},{4,36},{5,13},{6,38},{7,15},{8,40},{9,1... | collective-permute-start | bytes 884744 | tf_op jit(solution)/shard_map/ppermute | solution.py:41
  334.9 115.6 %collective-permute-start.11 = (bf16[144,1024]{1,0:T(8,128)(2,1)S(1)}, bf16[144,1024]{1,0:T(8,128)(2,1)S(1)}, u32[]{:S(2)}, u32[]{:S(2)}) collective-permute-start(bf16[144,1024]{1,0:T(8,128)(2,1)S(1)} %get-tuple-element.51), channel_id=1, source_target_pairs={{0,96},{1,25},{2,98},{3,27},{4,100},{5,29},{6,102},{7,31},{8,104},... | collective-permute-start | bytes 884744 | tf_op jit(solution)/shard_map/ppermute | solution.py:41
  368.7 81.8 %collective-permute-start.9 = (bf16[144,1024]{1,0:T(8,128)(2,1)S(1)}, bf16[144,1024]{1,0:T(8,128)(2,1)S(1)}, u32[]{:S(2)}, u32[]{:S(2)}) collective-permute-start(bf16[144,1024]{1,0:T(8,128)(2,1)S(1)} %far_last.1), channel_id=1, source_target_pairs={{0,64},{1,17},{2,66},{3,19},{4,68},{5,21},{6,70},{7,23},{8,72},{9,... | collective-permute-start | bytes 884744 | tf_op jit(solution)/shard_map/ppermute | solution.py:41

commit v2 on v1

--- a/solution.py
+++ b/solution.py
@@ -400,18 +400,18 @@
     first = prepare(
         "turn_keys_first",
         functools.partial(key_kernel, 0),
-        (2 * CHUNK, HEAD),
-        (k, v, positions),
-        [VMEM] * 3,
+        (PLACES + META, HEAD),
+        (k, v, positions, fk, fv, order, span),
+        [VMEM] * 6 + [pl.BlockSpec(memory_space=pltpu.SMEM)],
         2 * 10**9,
     )
     first_near = [shift(first, "keys", -1), shift(first, "keys", 1)]
     second = prepare(
         "turn_keys_second",
         functools.partial(key_kernel, CHUNK),
-        (PLACES + META, HEAD),
-        (k, v, positions, fk, fv, order, span),
-        [VMEM] * 6 + [pl.BlockSpec(memory_space=pltpu.SMEM)],
+        (2 * CHUNK, HEAD),
+        (k, v, positions),
+        [VMEM] * 3,
         2 * 10**9,
     )
     second_near = [shift(second, "keys", -1), shift(second, "keys", 1)]
@@ -425,7 +425,7 @@
     near = attend("near_near", q_near, [*first_near, *second_near], state, skip=1)
     far = attend("far_second", [q_far], second_near, far)
     near, far = lax.optimization_barrier((near, far))
-    fresh = [second, *second_near, second_far]
+    fresh = [first, *first_near, first_far]
     r_ahead, r_behind = attend("near_last", q_near, [first_far, second_far], near, fresh, finish=True)
     (r_far,) = attend("far_last", [q_far], [first_far, second_far], far, fresh, finish=True)
     back = [shift(r_far, "queries", 2), shift(r_ahead, "queries", 1), shift(r_behind, "queries", -1)]

time: 452 us -> 452 us (level)
  no operation moved by 1% of the time
where the time goes in v2:
time: 452 us
  Pallas kernels  430 us (95%)
  starting transfers between devices  18.4 us (4%)
    pallas_call x8, Pallas kernels, attend(): pl.pallas_call(functools.partial(attend_kernel, plan), out_shape=outs, in...  428 us
    ppermute x12, starting transfers between devices, shift(): return lax.ppermute(block, ('ctx', 'tp'), pairs)  18.4 us
  transfers between devices with their start and end apart: 12, of which 0 were waited for; matrix products, arithmetic and copies ran while one was open for 0% of the time, Pallas kernels for 81%

profile of v2, /device:TPU:0, one launch (start us, length us, event | category | flops | bytes accessed | tf_op | source)
XLA Modules:
  0.0 451.7 jit_solution(8686603919802369900)
XLA Ops:
  0.6 0.0 copy-start.6
  0.6 0.6 copy-done.6
  1.3 0.0 copy-start.2
  1.3 0.1 angles.1.angle_ref
  1.4 0.9 copy-done.2
  2.2 0.0 copy-start
  2.2 0.0 copy-start.1
  2.2 0.0 copy-start.3
  2.2 0.0 copy-start.4
  2.2 0.0 copy-start.5
  2.3 0.0 copy-start.7
  2.3 0.2 turn_queries.1.refs_0_
  2.4 4.0 collective-permute-start.4
  6.5 0.7 collective-permute-start.5
  7.2 1.3 collective-permute-start.6
  9.2 0.0 copy-done
  9.2 0.0 copy-done.1
  9.2 0.0 copy-done.3
  9.2 0.0 copy-done.4
  9.2 0.0 copy-done.5
  9.2 0.0 copy-done.7
  9.2 0.7 turn_keys_first.1.refs_3_.refs_1_.refs_7_.refs_4_
  10.0 1.6 collective-permute-start.1
  11.6 1.7 collective-permute-start
  13.3 0.7 turn_keys_second.1.refs_4_.refs_2_
  13.9 25.2 %mine_own.1 = (f32[1,128,1024]{2,1,0:T(8,128)S(1)}, f32[1,8,1024]{2,1,0:T(8,128)S(1)}) custom-call(bf16[144,1024]{1,0:T(8,128)(2,1)S(1)} %turn_queries.1.refs_0_, bf16[2320,128]{1,0:T(8,128)(2,1)S(1)} %turn_keys_first.1.refs_3_.refs_1_.refs_7_.refs_4_, bf16[2048,128]{1,0:T(8,128)(2,1)S(1)} %turn_keys_second.1.refs_4_.refs_2_), custom_call_target="tpu_custom_call" | custom-call | flops 2147483648 | tf_op jit(solution)/shard_map/mine_own/pallas_call | solution.py:346
  39.1 0.0 collective-permute-done.4.refs_0_
  39.1 1.9 collective-permute-start.2
  41.0 0.0 collective-permute-done.5.refs_1_.refs_0_
  41.0 0.2 collective-permute-start.3
  41.2 0.0 collective-permute-done.6.refs_2_.refs_1_
  41.2 75.5 %others_own.1 = (f32[3,128,1024]{2,1,0:T(8,128)S(1)}, f32[3,8,1024]{2,1,0:T(8,128)S(1)}) custom-call(bf16[144,1024]{1,0:T(8,128)(2,1)S(1)} %collective-permute-done.4.refs_0_, bf16[144,1024]{1,0:T(8,128)(2,1)S(1)} %collective-permute-done.5.refs_1_.refs_0_, bf16[144,1024]{1,0:T(8,128)(2,1)S(1)} %collective-permute-done.6.refs_2_.refs_1_, ...), custom_call_target="tpu_custom_call" | custom-call | flops 6442450944 | tf_op jit(solution)/shard_map/others_own/pallas_call | solution.py:346
  116.7 0.0 collective-permute-done.1.refs_2_.refs_9_.refs_3_.refs_5_.refs_6_
  116.7 0.0 collective-permute-done.refs_1_.refs_8_.refs_2_.refs_4_.refs_5_
  116.7 25.2 %far_first.1 = (f32[1,128,1024]{2,1,0:T(8,128)S(1)}, f32[1,8,1024]{2,1,0:T(8,128)S(1)}) custom-call(bf16[144,1024]{1,0:T(8,128)(2,1)S(1)} %collective-permute-done.4.refs_0_, bf16[2320,128]{1,0:T(8,128)(2,1)S(1)} %collective-permute-done.refs_1_.refs_8_.refs_2_.refs_4_.refs_5_, ...), custom_call_target="tpu_custom_call" | custom-call | flops 2147483648 | tf_op jit(solution)/shard_map/far_first/pallas_call | solution.py:346
  142.0 0.0 collective-permute-done.2.refs_3_.refs_4_.refs_1_
  142.0 0.4 collective-permute-start.7
  142.4 2.9 collective-permute-start.8
  145.3 0.0 collective-permute-done.3.refs_4_.refs_5_.refs_2_
  145.3 25.2 %far_second.1 = (f32[1,128,1024]{2,1,0:T(8,128)S(1)}, f32[1,8,1024]{2,1,0:T(8,128)S(1)}) custom-call(bf16[144,1024]{1,0:T(8,128)(2,1)S(1)} %collective-permute-done.4.refs_0_, bf16[2048,128]{1,0:T(8,128)(2,1)S(1)} %collective-permute-done.2.refs_3_.refs_4_.refs_1_, bf16[2048,128]{1,0:T(8,128)(2,1)S(1)} %collective-permute-done.3.refs_4_.refs_5_.refs_2_, ...), custom_call_target="tpu_custom_call" | custom-call | flops 2147483648 | tf_op jit(solution)/shard_map/far_second/pallas_call | solution.py:346
  170.6 100.2 %near_near.1 = (f32[2,128,1024]{2,1,0:T(8,128)S(1)}, f32[2,8,1024]{2,1,0:T(8,128)S(1)}) custom-call(bf16[144,1024]{1,0:T(8,128)(2,1)S(1)} %collective-permute-done.5.refs_1_.refs_0_, bf16[144,1024]{1,0:T(8,128)(2,1)S(1)} %collective-permute-done.6.refs_2_.refs_1_, bf16[2320,128]{1,0:T(8,128)(2,1)S(1)} %collective-permute-done.refs_1_.refs_8_.refs_2_.refs_4_.refs_5_, ...), custom_call_target="tpu_custom_call" | custom-call | flops 8589934592 | tf_op jit(solution)/shard_map/near_near/pallas_call | solution.py:346
  270.7 0.0 collective-permute-done.8.refs_6_.refs_2_.refs_3_
  270.8 0.0 collective-permute-done.7.refs_5_.refs_10_.refs_1_.refs_6_.refs_2_.refs_7_
  270.8 63.2 %near_last.1 = (bf16[144,1024]{1,0:T(8,128)(2,1)S(1)}, bf16[144,1024]{1,0:T(8,128)(2,1)S(1)}) custom-call(bf16[144,1024]{1,0:T(8,128)(2,1)S(1)} %collective-permute-done.5.refs_1_.refs_0_, bf16[144,1024]{1,0:T(8,128)(2,1)S(1)} %collective-permute-done.6.refs_2_.refs_1_, ...), custom_call_target="tpu_custom_call" | custom-call | flops 5368709120 | tf_op jit(solution)/shard_map/near_last/pallas_call | solution.py:346
  334.0 1.1 collective-permute-start.10
  335.1 2.2 collective-permute-start.11
  337.3 31.6 %far_last.1 = bf16[144,1024]{1,0:T(8,128)(2,1)S(1)} custom-call(bf16[144,1024]{1,0:T(8,128)(2,1)S(1)} %collective-permute-done.4.refs_0_, bf16[2320,128]{1,0:T(8,128)(2,1)S(1)} %collective-permute-done.7.refs_5_.refs_10_.refs_1_.refs_6_.refs_2_.refs_7_, bf16[2048,128]{1,0:T(8,128)(2,1)S(1)} %collective-permute-done.8.refs_6_.refs_2_.refs_3_, ...), custom_call_target="tpu_custom_call" | custom-call | flops 2684354560 | tf_op jit(solution)/shard_map/far_last/pallas_call | solution.py:346
  368.9 0.3 collective-permute-start.9
  369.1 81.5 %mine_rest.1 = (f32[1,128,1024]{2,1,0:T(8,128)S(1)}, f32[1,8,1024]{2,1,0:T(8,128)S(1)}) custom-call(bf16[144,1024]{1,0:T(8,128)(2,1)S(1)} %turn_queries.1.refs_0_, bf16[2320,128]{1,0:T(8,128)(2,1)S(1)} %collective-permute-done.refs_1_.refs_8_.refs_2_.refs_4_.refs_5_, bf16[2320,128]{1,0:T(8,128)(2,1)S(1)} %collective-permute-done.1.refs_2_.refs_9_.refs_3_.refs_5_.refs_6_, ...), custom_call_target="tpu_custom_call" | custom-call | flops 6979321856 | tf_op jit(solution)/shard_map/mine_rest/pallas_call | solution.py:346
  450.6 0.0 collective-permute-done.10.refs_1_
  450.6 0.0 collective-permute-done.11.refs_2_
  450.7 0.0 collective-permute-done.9.refs_0_
  450.7 1.0 combine.1
Async XLA Ops:
  0.6 0.7 copy-start.6
  1.3 0.9 copy-start.2
  2.2 6.9 %copy-start = (bf16[2048,128]{1,0:T(8,128)(2,1)S(1)}, bf16[2048,128]{1,0:T(8,128)(2,1)}, u32[]{:S(2)}) copy-start(bf16[2048,128]{1,0:T(8,128)(2,1)} %k_ref.3) | copy-start | bytes 1572868
  2.2 6.9 %copy-start.1 = (bf16[2048,128]{1,0:T(8,128)(2,1)S(1)}, bf16[2048,128]{1,0:T(8,128)(2,1)}, u32[]{:S(2)}) copy-start(bf16[2048,128]{1,0:T(8,128)(2,1)} %v_ref.3) | copy-start | bytes 1572868
  2.2 6.9 %copy-start.3 = (bf16[128,128]{1,0:T(8,128)(2,1)S(1)}, bf16[128,128]{1,0:T(8,128)(2,1)}, u32[]{:S(2)}) copy-start(bf16[128,128]{1,0:T(8,128)(2,1)} %refs_0_.1) | copy-start | bytes 98308
  2.2 7.0 %copy-start.4 = (bf16[128,128]{1,0:T(8,128)(2,1)S(1)}, bf16[128,128]{1,0:T(8,128)(2,1)}, u32[]{:S(2)}) copy-start(bf16[128,128]{1,0:T(8,128)(2,1)} %refs_1_.1) | copy-start | bytes 98308
  2.2 7.0 %copy-start.5 = (s32[2048]{0:T(1024)S(1)}, s32[2048]{0:T(1024)}, u32[]{:S(2)}) copy-start(s32[2048]{0:T(1024)} %param.13) | copy-start | bytes 24580
  2.3 7.0 %copy-start.7 = (s32[128]{0:T(128)S(1)}, s32[128]{0:T(128)}, u32[]{:S(2)}) copy-start(s32[128]{0:T(128)} %param.14) | copy-start | bytes 1540
  2.4 36.7 %collective-permute-start.4 = (bf16[144,1024]{1,0:T(8,128)(2,1)S(1)}, bf16[144,1024]{1,0:T(8,128)(2,1)S(1)}, u32[]{:S(2)}, u32[]{:S(2)}) collective-permute-start(bf16[144,1024]{1,0:T(8,128)(2,1)S(1)} %turn_queries.1.refs_0_), channel_id=1, source_target_pairs={{0,64},{1,17},{2,66},{3,19},{4,68},{5,21},{6,70},{7,23},{8,72},{9,... | collective-permute-start | bytes 884744 | tf_op jit(solution)/shard_map/ppermute | solution.py:41
  6.5 34.5 %collective-permute-start.5 = (bf16[144,1024]{1,0:T(8,128)(2,1)S(1)}, bf16[144,1024]{1,0:T(8,128)(2,1)S(1)}, u32[]{:S(2)}, u32[]{:S(2)}) collective-permute-start(bf16[144,1024]{1,0:T(8,128)(2,1)S(1)} %turn_queries.1.refs_0_), channel_id=1, source_target_pairs={{0,96},{1,25},{2,98},{3,27},{4,100},{5,29},{6,102},{7,31},{8,104},... | collective-permute-start | bytes 884744 | tf_op jit(solution)/shard_map/ppermute | solution.py:41
  7.2 34.0 %collective-permute-start.6 = (bf16[144,1024]{1,0:T(8,128)(2,1)S(1)}, bf16[144,1024]{1,0:T(8,128)(2,1)S(1)}, u32[]{:S(2)}, u32[]{:S(2)}) collective-permute-start(bf16[144,1024]{1,0:T(8,128)(2,1)S(1)} %turn_queries.1.refs_0_), channel_id=1, source_target_pairs={{0,32},{1,9},{2,34},{3,11},{4,36},{5,13},{6,38},{7,15},{8,40},{9,1... | collective-permute-start | bytes 884744 | tf_op jit(solution)/shard_map/ppermute | solution.py:41
  10.0 106.8 %collective-permute-start.1 = (bf16[2320,128]{1,0:T(8,128)(2,1)S(1)}, bf16[2320,128]{1,0:T(8,128)(2,1)S(1)}, u32[]{:S(2)}, u32[]{:S(2)}) collective-permute-start(bf16[2320,128]{1,0:T(8,128)(2,1)S(1)} %turn_keys_first.1.refs_3_.refs_1_.refs_7_.refs_4_), channel_id=1, source_target_pairs={{0,8},{1,33},{2,10},{3,35},{4,12},{5,37},{6,14},{7,39},{8,16},{9,4... | collective-permute-start | bytes 1781768 | tf_op jit(solution)/shard_map/ppermute | solution.py:41
  11.6 105.1 %collective-permute-start = (bf16[2320,128]{1,0:T(8,128)(2,1)S(1)}, bf16[2320,128]{1,0:T(8,128)(2,1)S(1)}, u32[]{:S(2)}, u32[]{:S(2)}) collective-permute-start(bf16[2320,128]{1,0:T(8,128)(2,1)S(1)} %turn_keys_first.1.refs_3_.refs_1_.refs_7_.refs_4_), channel_id=1, source_target_pairs={{0,24},{1,97},{2,26},{3,99},{4,28},{5,101},{6,30},{7,103},{8,0},{9... | collective-permute-start | bytes 1781768 | tf_op jit(solution)/shard_map/ppermute | solution.py:41
  39.1 102.8 %collective-permute-start.2 = (bf16[2048,128]{1,0:T(8,128)(2,1)S(1)}, bf16[2048,128]{1,0:T(8,128)(2,1)S(1)}, u32[]{:S(2)}, u32[]{:S(2)}) collective-permute-start(bf16[2048,128]{1,0:T(8,128)(2,1)S(1)} %turn_keys_second.1.refs_4_.refs_2_), channel_id=1, source_target_pairs={{0,24},{1,97},{2,26},{3,99},{4,28},{5,101},{6,30},{7,103},{8,0},{9... | collective-permute-start | bytes 1572872 | tf_op jit(solution)/shard_map/ppermute | solution.py:41
  41.0 104.3 %collective-permute-start.3 = (bf16[2048,128]{1,0:T(8,128)(2,1)S(1)}, bf16[2048,128]{1,0:T(8,128)(2,1)S(1)}, u32[]{:S(2)}, u32[]{:S(2)}) collective-permute-start(bf16[2048,128]{1,0:T(8,128)(2,1)S(1)} %turn_keys_second.1.refs_4_.refs_2_), channel_id=1, source_target_pairs={{0,8},{1,33},{2,10},{3,35},{4,12},{5,37},{6,14},{7,39},{8,16},{9,4... | collective-permute-start | bytes 1572872 | tf_op jit(solution)/shard_map/ppermute | solution.py:41
  142.0 128.8 %collective-permute-start.7 = (bf16[2320,128]{1,0:T(8,128)(2,1)S(1)}, bf16[2320,128]{1,0:T(8,128)(2,1)S(1)}, u32[]{:S(2)}, u32[]{:S(2)}) collective-permute-start(bf16[2320,128]{1,0:T(8,128)(2,1)S(1)} %collective-permute-done.1.refs_2_.refs_9_.refs_3_.refs_5_.refs_6_), channel_id=1, source_target_pairs={{0,8},{1,33},{2,10},{3,35},{4,12},{5,37},{6,14},{7,39},{8,16},{9,4... | collective-permute-start | bytes 1781768 | tf_op jit(solution)/shard_map/ppermute | solution.py:41
  142.4 128.3 %collective-permute-start.8 = (bf16[2048,128]{1,0:T(8,128)(2,1)S(1)}, bf16[2048,128]{1,0:T(8,128)(2,1)S(1)}, u32[]{:S(2)}, u32[]{:S(2)}) collective-permute-start(bf16[2048,128]{1,0:T(8,128)(2,1)S(1)} %collective-permute-done.2.refs_3_.refs_4_.refs_1_), channel_id=1, source_target_pairs={{0,24},{1,97},{2,26},{3,99},{4,28},{5,101},{6,30},{7,103},{8,0},{9... | collective-permute-start | bytes 1572872 | tf_op jit(solution)/shard_map/ppermute | solution.py:41
  334.0 116.7 %collective-permute-start.10 = (bf16[144,1024]{1,0:T(8,128)(2,1)S(1)}, bf16[144,1024]{1,0:T(8,128)(2,1)S(1)}, u32[]{:S(2)}, u32[]{:S(2)}) collective-permute-start(bf16[144,1024]{1,0:T(8,128)(2,1)S(1)} %get-tuple-element.50), channel_id=1, source_target_pairs={{0,32},{1,9},{2,34},{3,11},{4,36},{5,13},{6,38},{7,15},{8,40},{9,1... | collective-permute-start | bytes 884744 | tf_op jit(solution)/shard_map/ppermute | solution.py:41
  335.1 115.6 %collective-permute-start.11 = (bf16[144,1024]{1,0:T(8,128)(2,1)S(1)}, bf16[144,1024]{1,0:T(8,128)(2,1)S(1)}, u32[]{:S(2)}, u32[]{:S(2)}) collective-permute-start(bf16[144,1024]{1,0:T(8,128)(2,1)S(1)} %get-tuple-element.51), channel_id=1, source_target_pairs={{0,96},{1,25},{2,98},{3,27},{4,100},{5,29},{6,102},{7,31},{8,104},... | collective-permute-start | bytes 884744 | tf_op jit(solution)/shard_map/ppermute | solution.py:41
  368.9 81.8 %collective-permute-start.9 = (bf16[144,1024]{1,0:T(8,128)(2,1)S(1)}, bf16[144,1024]{1,0:T(8,128)(2,1)S(1)}, u32[]{:S(2)}, u32[]{:S(2)}) collective-permute-start(bf16[144,1024]{1,0:T(8,128)(2,1)S(1)} %far_last.1), channel_id=1, source_target_pairs={{0,64},{1,17},{2,66},{3,19},{4,68},{5,21},{6,70},{7,23},{8,72},{9,... | collective-permute-start | bytes 884744 | tf_op jit(solution)/shard_map/ppermute | solution.py:41
